TPU v7x, 32 devices: a whole 2x2x4 slice. The times are simulated.
32 devices in a mesh: gx: 16 (over z, y, core), gz: 2 (over x).
Axes of the slice: x: 2, y: 2, z: 4, core: 2. Of those that a mesh axis runs over, the one named last changes fastest.
Arguments:
- strain_inc: float32 [6, 32, 256, 256], P(None, 'gx', None, 'gz'), may hold values from -2.5 to 2.5
- stress_old: float32 [6, 32, 256, 256], P(None, 'gx', None, 'gz'), may hold values from -6 to 6
- material_id: int32 [32, 256, 256], P('gx', None, 'gz'), may hold values from 0 to 7
- cohesion: float32 [8], replicated, may hold values from 1 to 4
- friction: float32 [8], replicated, may hold values from 0.05 to 0.3
- pressure: float32 [32, 256, 256], P('gx', 'gz'), may hold values from -6 to 6
- storage: float32 [32, 256, 256], P('gx', 'gz'), may hold values from 0.5 to 4
- perm_class: int32 [32, 256, 256], P('gx', 'gz'), may hold values from 0 to 15
- perm_table: float32 [16], replicated, may hold values from 0.5 to 8
Outputs:
- pressure_next: float32 [32, 256, 256], P('gx', 'gz')
- stress_next: float32 [6, 32, 256, 256], P(None, 'gx', None, 'gz')
- node_force: float32 [3, 32, 256, 256], P(None, 'gx', None, 'gz')
All inputs are finite; a program needn't handle non-finite values.
Results may differ from a plain program's by a relative error of at most 0.00002.
Values sent between devices are 32-bit elements; how exact they have to be, the bound alone decides.
A program may use at most 64 MiB of HBM per device.

v0:
```python
import jax
import jax.numpy as jnp
from jax import lax
from jax.sharding import PartitionSpec as P

BIOT = 0.8
SHEAR = 1.0
BULK = 1.5
FLOOR = 0.25
TINY = 1e-30


def extended(array, sides, width):
    for axis, dim in sides:
        count, length = (lax.axis_size(axis), array.shape[dim])
        up = [(i, (i + 1) % count) for i in range(count - 1)]
        down = [(j, i) for i, j in up]
        last = lax.slice_in_dim(array, length - width, length, axis=dim)
        leading = lax.slice_in_dim(array, 0, width, axis=dim)
        before = lax.ppermute(last, axis, up)
        after = lax.ppermute(leading, axis, down)
        array = jnp.concatenate([before, array, after], axis=dim)
    return array


def passed_along(block, axis, distance):
    devices = range(lax.axis_size(axis))
    route = [(i - distance, i) for i in devices if i - distance in devices]
    return lax.ppermute(block, axis, route)


def lookup(ids, table):
    result = jnp.zeros(ids.shape, jnp.float32)
    for entry in range(table.shape[0]):
        result = result + jnp.where(ids == entry, table[entry], jnp.zeros((), jnp.float32))
    return result


def neighbours():
    inner = slice(1, -1)
    return [
        (slice(2, None), inner, inner),
        (slice(0, -2), inner, inner),
        (inner, slice(2, None), inner),
        (inner, slice(0, -2), inner),
        (inner, inner, slice(2, None)),
        (inner, inner, slice(0, -2)),
    ]


def relax_padded(pressure_pad, cond_pad, storage, source):
    conduct = cond_pad[1:-1, 1:-1, 1:-1]
    numerator = source
    denominator = storage
    for offset in neighbours():
        cond_near = cond_pad[offset]
        transmit = 2.0 * conduct * cond_near / jnp.maximum(conduct + cond_near, TINY)
        numerator = numerator + transmit * pressure_pad[offset]
        denominator = denominator + transmit
    denominator = jnp.where(denominator > 0.0, denominator, jnp.ones((), jnp.float32))
    return numerator / denominator


def plastic(strain_inc, stress_old, material_id, cohesion, friction):
    normal_mask = jnp.array([1.0, 1.0, 1.0, 0.0, 0.0, 0.0], jnp.float32).reshape(6, 1, 1, 1)
    volume = strain_inc[0] + strain_inc[1] + strain_inc[2]
    trial_stress = (
        stress_old
        + 2.0 * SHEAR * (strain_inc - normal_mask * (volume / 3.0))
        + BULK * volume * normal_mask
    )
    first_invariant = trial_stress[0] + trial_stress[1] + trial_stress[2]
    deviator = trial_stress - normal_mask * (first_invariant / 3.0)
    second_invariant = 0.5 * (
        deviator[0] * deviator[0] + deviator[1] * deviator[1] + deviator[2] * deviator[2]
    )
    second_invariant = (
        second_invariant
        + deviator[3] * deviator[3]
        + deviator[4] * deviator[4]
        + deviator[5] * deviator[5]
    )
    equiv_shear = jnp.sqrt(second_invariant)
    strength = lookup(material_id, cohesion)
    slope = lookup(material_id, friction)
    yield_value = equiv_shear + slope * first_invariant - strength
    multiplier = jnp.maximum(yield_value, 0.0) / (SHEAR + 9.0 * BULK * slope * slope)
    shrink_factor = jnp.maximum(1.0 - SHEAR * multiplier / jnp.maximum(equiv_shear, FLOOR), 0.0)
    new_invariant = first_invariant - 9.0 * BULK * slope * multiplier
    return deviator * shrink_factor + normal_mask * (new_invariant / 3.0)


def corner_terms(stress_next, pressure_block):
    normal_mask = jnp.array([1.0, 1.0, 1.0, 0.0, 0.0, 0.0], jnp.float32).reshape(6, 1, 1, 1)
    total = stress_next - BIOT * pressure_block * normal_mask
    col_x = jnp.stack([total[0], total[3], total[5]])
    col_y = jnp.stack([total[3], total[1], total[4]])
    col_z = jnp.stack([total[5], total[4], total[2]])
    return (col_x, col_y, col_z)


def place_corner(term, along_x, along_y):
    placed = jnp.pad(term, ((0, 0), (along_x, 1 - along_x), (0, 0), (0, 0)))
    if along_y == 1:
        placed = jnp.pad(placed, ((0, 0), (0, 0), (1, 0), (0, 0)))[:, :, :-1]
    return placed


def node_parts(col_x, col_y, col_z):
    lower = None
    upper = None
    for corner in range(8):
        along_x = corner & 1
        along_y = corner >> 1 & 1
        along_z = corner >> 2
        term = 0.25 * (
            (2 * along_x - 1) * col_x + (2 * along_y - 1) * col_y + (2 * along_z - 1) * col_z
        )
        placed = place_corner(term, along_x, along_y)
        if along_z == 0:
            lower = placed if lower is None else lower + placed
        else:
            upper = placed if upper is None else upper + placed
    node_main = lower + jnp.pad(upper[..., :-1], ((0, 0), (0, 0), (0, 0), (1, 0)))
    node_rim = upper[..., -1]
    return (node_main, node_rim)


def on_device(
    strain_inc,
    stress_old,
    material_id,
    cohesion,
    friction,
    pressure,
    storage,
    perm_class,
    perm_table,
):
    strain_rate = strain_inc[0] + strain_inc[1] + strain_inc[2]
    rate_column = lax.all_to_all(strain_rate, "gz", split_axis=1, concat_axis=2, tiled=True)
    stress_next = plastic(strain_inc, stress_old, material_id, cohesion, friction)
    conduct = lookup(perm_class, perm_table)
    source = storage * pressure - BIOT * rate_column
    pressure_pair = extended(jnp.stack([pressure, conduct]), (("gx", 1), ("gz", 2)), 1)
    pressure_pair = jnp.pad(pressure_pair, ((0, 0), (0, 0), (0, 0), (1, 1)))
    first_sweep = relax_padded(pressure_pair[0], pressure_pair[1], storage, source)
    bordered = extended(first_sweep, (("gx", 0), ("gz", 1)), 1)
    bordered = jnp.pad(bordered, ((0, 0), (0, 0), (1, 1)))
    pressure_next = relax_padded(bordered, pressure_pair[1], storage, source)
    pressure_block = lax.all_to_all(pressure_next, "gz", split_axis=2, concat_axis=1, tiled=True)
    col_x, col_y, col_z = corner_terms(stress_next, pressure_block)
    node_main, node_rim = node_parts(col_x, col_y, col_z)
    from_below = passed_along(node_rim, "gz", 1)
    node_main = node_main.at[:, :, :, 0].add(from_below)
    slab_plane = passed_along(node_main[:, -1], "gx", 1)
    node_main = node_main.at[:, 0].add(slab_plane)
    node_force = node_main[:, :-1]
    return (pressure_next, stress_next, node_force)


def solution(mesh):
    in_specs = (
        P(None, "gx", None, "gz"),
        P(None, "gx", None, "gz"),
        P("gx", None, "gz"),
        P(),
        P(),
        P("gx", "gz", None),
        P("gx", "gz", None),
        P("gx", "gz", None),
        P(),
    )
    out_specs = (P("gx", "gz", None), P(None, "gx", None, "gz"), P(None, "gx", None, "gz"))
    return jax.shard_map(
        on_device, mesh=mesh, in_specs=in_specs, out_specs=out_specs, check_vma=False
    )
```

profile of v0, /device:TPU:10, one launch (start us, length us, event | category | flops | bytes accessed | tf_op | source)
XLA Modules:
  0.0 118.8 jit_solution(4340846625910367335)
XLA Ops:
  0.6 1.9 %fusion.46 = (f32[1]{0:T(128)}, f32[1]{0:T(128)}, f32[1]{0:T(128)}, f32[1]{0:T(128)}, f32[1]{0:T(128)}, /*index=5*/f32[1]{0:T(128)}, f32[1]{0:T(128)}, f32[1]{0:...) fusion(f32[16]{0:T(128)} %param.23), kind=kLoop, calls=%fused_computation.149 | loop fusion | bytes 128 | tf_op jit(solution)/shard_map/slice | solution.py:35
  2.6 12.0 %add_bitcast_fusion = f32[1,2,128,256]{3,2,1,0:T(8,128)} fusion(s32[2,128,256]{2,1,0:T(8,128)} %param.22, f32[]{:T(128)} %bitcast.19, f32[]{:T(128)} %bitcast.18, f32[]{:T(128)} %bitcast.17, f32[]{:T(128)} %bitcast.16, f32[]{:T(128)} %bitcast.15, f32[]{:T(128)} %bitcast.14, f32[]{:T(128)} %bitcast.13, f32[]{:T(128)} %bitcast.12, f32[]{:T(128)} %bitcast.11, ...), kind=kLoop, calls=%fused_computation.125 | loop fusion | flops 3080192 | bytes 524352 | tf_op jit(solution)/shard_map/stack | solution.py:145
  14.6 1.9 %fusion.11 = (f32[2,1,128,256]{3,2,1,0:T(8,128)}, f32[2,1,128,256]{3,2,1,0:T(8,128)}) fusion(f32[1,2,128,256]{3,2,1,0:T(8,128)} %bitcast.79, f32[1,2,128,256]{3,2,1,0:T(8,128)} %add_bitcast_fusion), kind=kLoop, calls=%fused_computation.57 | loop fusion | flops 131072 | bytes 1048576 | tf_op jit(solution)/shard_map/stack | solution.py:145
  16.5 2.0 %collective-permute-start = (f32[2,1,128,256]{3,2,1,0:T(8,128)}, f32[2,1,128,256]{3,2,1,0:T(8,128)}, u32[]{:S(2)}, u32[]{:S(2)}) collective-permute-start(f32[2,1,128,256]{3,2,1,0:T(8,128)} %get-tuple-element.84), channel_id=1, source_target_pairs={{0,2},{2,4},{4,6},{6,8},{8,10},{10,12},{12,14},{14,16},{16,18},{18... | collective-permute-start | bytes 786440 | tf_op jit(solution)/shard_map/ppermute | solution.py:20
  18.6 4.5 %collective-permute-start.1 = (f32[2,1,128,256]{3,2,1,0:T(8,128)}, f32[2,1,128,256]{3,2,1,0:T(8,128)}, u32[]{:S(2)}, u32[]{:S(2)}) collective-permute-start(f32[2,1,128,256]{3,2,1,0:T(8,128)} %get-tuple-element.85), channel_id=1, source_target_pairs={{2,0},{4,2},{6,4},{8,6},{10,8},{12,10},{14,12},{16,14},{18,16},{20... | collective-permute-start | bytes 786440 | tf_op jit(solution)/shard_map/ppermute | solution.py:21
  23.2 0.9 copy.250
  24.1 4.6 %all-to-all-start = ((f32[2,256,128]{2,0,1:T(2,128)}), f32[2,256,128]{2,0,1:T(2,128)}, u32[]{:S(2)}, u32[]{:S(2)}) async-start(f32[2,256,128]{2,0,1:T(2,128)} %copy.250), calls=%async_computation | async-start | bytes 524288 | tf_op jit(solution)/shard_map/all_to_all | solution.py:141
  28.8 1.8 %multiply_add_fusion.1 = f32[6,2,256,128]{3,2,1,0:T(8,128)S(1)} fusion(f32[6,2,256,128]{3,2,1,0:T(8,128)} %param.16, f32[6,2,256,128]{3,2,1,0:T(8,128)S(1)} %copy-done.1, f32[2,256,128]{2,1,0:T(8,128)S(1)} %multiply_bitcast_fusion.1, f32[2,256,128]{2,1,0:T(8,128)S(1)} %get-tuple-element.62, f32[6]{0:T(128)S(1)} %copy-done.18), kind=kLoop, calls=%fused_computation.11 | loop fusion | flops 2359296 | bytes 5242904 | tf_op jit(solution)/shard_map/add | solution.py:68
  30.5 0.8 multiply_bitcast_fusion
  31.3 0.2 multiply_subtract_fusion.1
  31.6 0.5 copy-done.2
  32.0 0.0 collective-permute-done
  32.0 0.0 collective-permute-done.1
  32.0 0.3 copy-done
  32.4 0.8 pad_maximum_fusion.15
  33.2 1.3 %collective-permute-start.2 = (f32[2,4,1,256]{3,1,2,0:T(4,128)S(1)}, f32[2,4,1,256]{3,1,2,0:T(4,128)S(1)}, u32[]{:S(2)}, u32[]{:S(2)}) collective-permute-start(f32[2,4,1,256]{3,1,2,0:T(4,128)S(1)} %copy.252), channel_id=1, source_target_pairs={{0,1},{2,3},{4,5},{6,7},{8,9},{10,11},{12,13},{14,15},{16,17},{18,... | collective-permute-start | bytes 24584 | tf_op jit(solution)/shard_map/ppermute | solution.py:20
  34.5 4.5 %collective-permute-start.3 = (f32[2,4,1,256]{3,1,2,0:T(4,128)S(1)}, f32[2,4,1,256]{3,1,2,0:T(4,128)S(1)}, u32[]{:S(2)}, u32[]{:S(2)}) collective-permute-start(f32[2,4,1,256]{3,1,2,0:T(4,128)S(1)} %copy.253), channel_id=1, source_target_pairs={{1,0},{3,2},{5,4},{7,6},{9,8},{11,10},{13,12},{15,14},{17,16},{19,... | collective-permute-start | bytes 24584 | tf_op jit(solution)/shard_map/ppermute | solution.py:21
  39.1 1.1 broadcast_multiply_fusion.1
  40.2 0.9 copy.261
  41.1 1.9 %mul.296 = f32[2,128,256]{2,1,0:T(8,128)} reshape(f32[2,128,2,128]{3,2,1,0:T(2,128)} %bitcast.85) | data formatting | bytes 524288 | tf_op jit(solution)/shard_map/mul | solution.py:144
  42.9 0.0 collective-permute-done.2
  42.9 0.0 collective-permute-done.3
  43.0 1.7 %select_maximum_fusion = f32[2,4,130,258]{3,2,1,0:T(8,128)S(1)} fusion(f32[2,4,1,256]{3,2,1,0:T(1,128)S(1)} %copy.255, f32[2,4,1,256]{3,2,1,0:T(1,128)S(1)} %copy.254, f32[2,1,128,256]{3,2,1,0:T(8,128)} %collective-permute-done.1, f32[2,1,128,256]{3,2,1,0:T(8,128)} %collective-permute-done, f32[1,2,128,256]{3,2,1,0:T(8,128)} %add_bitcast_fusion, ...), kind=kLoop, calls=%fused_computation.2 | loop fusion | flops 3756480 | bytes 2138240 | tf_op jit(solution)/shard_map/concatenate | solution.py:22
  44.7 0.0 copy-start.6
  44.7 0.0 copy-start.9
  44.7 0.1 slice_bitcast_fusion.1
  44.8 0.8 copy-done.6
  45.6 0.1 copy-done.9
  45.7 0.9 fusion.32
  46.7 1.9 %collective-permute-start.4 = (f32[1,128,256]{2,1,0:T(8,128)S(1)}, f32[1,128,256]{2,1,0:T(8,128)S(1)}, u32[]{:S(2)}, u32[]{:S(2)}) collective-permute-start(f32[1,128,256]{2,1,0:T(8,128)S(1)} %get-tuple-element.87), channel_id=1, source_target_pairs={{2,0},{4,2},{6,4},{8,6},{10,8},{12,10},{14,12},{16,14},{18,16},{20... | collective-permute-start | bytes 393224 | tf_op jit(solution)/shard_map/ppermute | solution.py:21
  48.6 2.4 %collective-permute-start.5 = (f32[1,128,256]{2,1,0:T(8,128)S(1)}, f32[1,128,256]{2,1,0:T(8,128)S(1)}, u32[]{:S(2)}, u32[]{:S(2)}) collective-permute-start(f32[1,128,256]{2,1,0:T(8,128)S(1)} %get-tuple-element.86), channel_id=1, source_target_pairs={{0,2},{2,4},{4,6},{6,8},{8,10},{10,12},{12,14},{14,16},{16,18},{18... | collective-permute-start | bytes 393224 | tf_op jit(solution)/shard_map/ppermute | solution.py:20
  51.0 0.7 fusion.44
  51.7 0.7 fusion.45
  52.4 3.4 %collective-permute-done.5 = f32[1,128,256]{2,1,0:T(8,128)S(1)} collective-permute-done((f32[1,128,256]{2,1,0:T(8,128)S(1)}, f32[1,128,256]{2,1,0:T(8,128)S(1)}, u32[]{:S(2)}, u32[]{:S(2)}) %collective-permute-start.5) | collective-permute-done | bytes 131104 | tf_op jit(solution)/shard_map/ppermute | solution.py:20
  55.8 1.6 %collective-permute-start.6 = (f32[4,1,256]{2,1,0:T(1,128)S(1)}, f32[4,1,256]{2,1,0:T(1,128)S(1)}, u32[]{:S(2)}, u32[]{:S(2)}) collective-permute-start(f32[4,1,256]{2,1,0:T(1,128)S(1)} %get-tuple-element.83), channel_id=1, source_target_pairs={{1,0},{3,2},{5,4},{7,6},{9,8},{11,10},{13,12},{15,14},{17,16},{19,... | collective-permute-start | bytes 12296 | tf_op jit(solution)/shard_map/ppermute | solution.py:21
  57.4 1.3 %collective-permute-start.7 = (f32[4,1,256]{2,1,0:T(1,128)S(1)}, f32[4,1,256]{2,1,0:T(1,128)S(1)}, u32[]{:S(2)}, u32[]{:S(2)}) collective-permute-start(f32[4,1,256]{2,1,0:T(1,128)S(1)} %get-tuple-element.82), channel_id=1, source_target_pairs={{0,1},{2,3},{4,5},{6,7},{8,9},{10,11},{12,13},{14,15},{16,17},{18,... | collective-permute-start | bytes 12296 | tf_op jit(solution)/shard_map/ppermute | solution.py:20
  58.8 11.5 %subtract_maximum_fusion = (f32[2,256,128]{2,1,0:T(8,128)}, f32[2,256,128]{2,1,0:T(8,128)}, pred[2,256,128]{2,1,0:T(8,128)(4,1)S(1)}, pred[2,256,128]{2,1,0:T(8,...) fusion(f32[]{:T(128)} %bitcast.43, f32[]{:T(128)} %bitcast.42, ...), kind=kLoop, calls=%fused_computation.114 | loop fusion | flops 4063232 | bytes 3145792 | tf_op jit(solution)/shard_map/max | solution.py:88
  70.3 0.3 select_maximum_fusion.5
  70.7 0.8 fusion.21
  71.5 0.0 copy-start.10
  71.5 0.7 copy-done.10
  72.2 0.8 copy.256
  73.0 6.2 %all-to-all-start.1 = ((f32[2,128,256]{1,0,2:T(2,128)}), f32[2,128,256]{1,0,2:T(2,128)S(1)}, u32[]{:S(2)}, u32[]{:S(2)}) async-start(f32[2,128,256]{1,0,2:T(2,128)} %copy.256), calls=%async_computation.1 | async-start | bytes 524288 | tf_op jit(solution)/shard_map/all_to_all | solution.py:151
  79.2 11.2 %fusion.10 = f32[2,256,128]{2,1,0:T(8,128)S(1)} fusion(f32[1,2,256,128]{3,2,1,0:T(8,128)S(1)} %copy-done.5, pred[2,256,128]{2,1,0:T(8,128)(4,1)} %get-tuple-element.59, f32[]{:T(128)} %bitcast.43, pred[2,256,128]{2,1,0:T(8,128)(4,1)} %get-tuple-element.58, f32[]{:T(128)} %bitcast.42, pred[2,256,128]{2,1,0:T(8,128)(4,1)S(1)} %copy-done.15, f32[]{:T(128)} %bitcast.41, ...), kind=kLoop, calls=%fused_computation.56 | loop fusion | flops 2686976 | bytes 1310784 | tf_op jit(solution)/shard_map/div | solution.py:90
  90.4 0.1 broadcast_multiply_fusion
  90.6 0.1 copy.257
  90.8 1.6 %multiply_subtract_fusion = (f32[6,2,256,128]{3,2,1,0:T(8,128)S(1)}, f32[6,2,256,128]{3,2,1,0:T(8,128)}) fusion(f32[2,256,128]{2,1,0:T(8,128)S(1)} %bitcast.83, f32[6]{0:T(128)S(1)} %copy-done.18, f32[2,256,128]{2,1,0:T(8,128)S(1)} %fusion.10, f32[2,256,128]{2,1,0:T(8,128)S(1)} %copy-done.7, f32[6,2,256,128]{3,2,1,0:T(8,128)S(1)} %multiply_add_fusion.1, ...), kind=kLoop, calls=%fused_computation.8 | loop fusion | flops 2752512 | bytes 5767192 | tf_op jit(solution)/shard_map/sub | solution.py:95
  92.3 0.1 fusion.42
  92.5 0.2 add_multiply_fusion.7
  92.6 0.2 add_multiply_fusion.6
  92.8 0.2 add_multiply_fusion
  93.0 0.2 add_multiply_fusion.4
  93.3 0.2 fusion.5
  93.4 0.7 slice_reduce_fusion
  94.2 1.3 %collective-permute-start.8 = (f32[3,3,256]{2,1,0:T(4,128)S(1)}, f32[3,3,256]{2,1,0:T(4,128)S(1)}, u32[]{:S(2)}, u32[]{:S(2)}) collective-permute-start(f32[3,3,256]{2,1,0:T(4,128)S(1)} %slice_reduce_fusion), channel_id=1, source_target_pairs={{0,1},{2,3},{4,5},{6,7},{8,9},{10,11},{12,13},{14,15},{16,17},{18,... | collective-permute-start | bytes 27656 | tf_op jit(solution)/shard_map/ppermute | solution.py:29
  95.5 0.5 fusion.3
  96.0 3.8 %collective-permute-done.8 = f32[3,3,256]{2,1,0:T(4,128)S(1)} collective-permute-done((f32[3,3,256]{2,1,0:T(4,128)S(1)}, f32[3,3,256]{2,1,0:T(4,128)S(1)}, u32[]{:S(2)}, u32[]{:S(2)}) %collective-permute-start.8) | collective-permute-done | bytes 9248 | tf_op jit(solution)/shard_map/ppermute | solution.py:29
  99.7 0.4 copy.258
  100.2 0.1 slice_add_fusion
  100.3 7.5 %scatter-add.6 = f32[3,3,256,128]{3,2,1,0:T(8,128)S(1)} dynamic-update-slice(f32[3,3,256,128]{3,2,1,0:T(8,128)S(1)} %fusion.3, f32[3,3,256,1]{3,2,1,0:T(8,128)S(1)} %slice_add_fusion, s32[]{:T(128)} %constant.100.clone.1, s32[]{:T(128)} %constant.100.clone.1, s32[]{:T(128)} %constant.100.clone.1, s32[]{:T(128)} %constant.100.clone.1) | dynamic-update-slice | bytes 18436 | tf_op jit(solution)/shard_map/scatter-add | solution.py:155
  107.8 1.9 %collective-permute-start.9 = (f32[3,256,128]{2,1,0:T(8,128)S(1)}, f32[3,256,128]{2,1,0:T(8,128)S(1)}, u32[]{:S(2)}, u32[]{:S(2)}) collective-permute-start(f32[3,256,128]{2,1,0:T(8,128)S(1)} %slice_bitcast_fusion.2), channel_id=1, source_target_pairs={{0,2},{2,4},{4,6},{6,8},{8,10},{10,12},{12,14},{14,16},{16,18},{18... | collective-permute-start | bytes 1179656 | tf_op jit(solution)/shard_map/ppermute | solution.py:29
  109.7 8.1 %collective-permute-done.9 = f32[3,256,128]{2,1,0:T(8,128)S(1)} collective-permute-done((f32[3,256,128]{2,1,0:T(8,128)S(1)}, f32[3,256,128]{2,1,0:T(8,128)S(1)}, u32[]{:S(2)}, u32[]{:S(2)}) %collective-permute-start.9) | collective-permute-done | bytes 393248 | tf_op jit(solution)/shard_map/ppermute | solution.py:29
  117.8 0.1 fusion.7
  117.9 0.9 slice.475
  (44 shorter events, 0.2 us)
Async XLA Ops:
  0.6 22.5 %copy-start.1 = (f32[6,2,256,128]{3,2,1,0:T(8,128)S(1)}, f32[6,2,256,128]{3,2,1,0:T(8,128)}, u32[]{:S(2)}) copy-start(f32[6,2,256,128]{3,2,1,0:T(8,128)} %param.15) | copy-start | bytes 4718596
  16.5 12.2 %copy-start.18 = (f32[6]{0:T(128)S(1)}, f32[6]{0:T(128)}, u32[]{:S(2)}) copy-start(f32[6]{0:T(128)} %constant.126.clone) | copy-start | bytes 76
  16.5 15.5 %collective-permute-start = (f32[2,1,128,256]{3,2,1,0:T(8,128)}, f32[2,1,128,256]{3,2,1,0:T(8,128)}, u32[]{:S(2)}, u32[]{:S(2)}) collective-permute-start(f32[2,1,128,256]{3,2,1,0:T(8,128)} %get-tuple-element.84), channel_id=1, source_target_pairs={{0,2},{2,4},{4,6},{6,8},{8,10},{10,12},{12,14},{14,16},{16,18},{18... | collective-permute-start | bytes 786440 | tf_op jit(solution)/shard_map/ppermute | solution.py:20
  18.6 13.5 %collective-permute-start.1 = (f32[2,1,128,256]{3,2,1,0:T(8,128)}, f32[2,1,128,256]{3,2,1,0:T(8,128)}, u32[]{:S(2)}, u32[]{:S(2)}) collective-permute-start(f32[2,1,128,256]{3,2,1,0:T(8,128)} %get-tuple-element.85), channel_id=1, source_target_pairs={{2,0},{4,2},{6,4},{8,6},{10,8},{12,10},{14,12},{16,14},{18,16},{20... | collective-permute-start | bytes 786440 | tf_op jit(solution)/shard_map/ppermute | solution.py:21
  24.1 14.9 %all-to-all-start = ((f32[2,256,128]{2,0,1:T(2,128)}), f32[2,256,128]{2,0,1:T(2,128)}, u32[]{:S(2)}, u32[]{:S(2)}) async-start(f32[2,256,128]{2,0,1:T(2,128)} %copy.250), calls=%async_computation | async-start | bytes 524288 | tf_op jit(solution)/shard_map/all_to_all | solution.py:141
  31.3 0.7 copy-start.2
  31.3 1.0 copy-start
  33.2 9.7 %collective-permute-start.2 = (f32[2,4,1,256]{3,1,2,0:T(4,128)S(1)}, f32[2,4,1,256]{3,1,2,0:T(4,128)S(1)}, u32[]{:S(2)}, u32[]{:S(2)}) collective-permute-start(f32[2,4,1,256]{3,1,2,0:T(4,128)S(1)} %copy.252), channel_id=1, source_target_pairs={{0,1},{2,3},{4,5},{6,7},{8,9},{10,11},{12,13},{14,15},{16,17},{18,... | collective-permute-start | bytes 24584 | tf_op jit(solution)/shard_map/ppermute | solution.py:20
  34.5 8.4 %collective-permute-start.3 = (f32[2,4,1,256]{3,1,2,0:T(4,128)S(1)}, f32[2,4,1,256]{3,1,2,0:T(4,128)S(1)}, u32[]{:S(2)}, u32[]{:S(2)}) collective-permute-start(f32[2,4,1,256]{3,1,2,0:T(4,128)S(1)} %copy.253), channel_id=1, source_target_pairs={{1,0},{3,2},{5,4},{7,6},{9,8},{11,10},{13,12},{15,14},{17,16},{19,... | collective-permute-start | bytes 24584 | tf_op jit(solution)/shard_map/ppermute | solution.py:21
  44.7 1.0 copy-start.6
  44.7 1.0 copy-start.9
  45.7 5.3 %copy-start.16 = (f32[8]{0:T(128)S(1)}, f32[8]{0:T(128)}, u32[]{:S(2)}) copy-start(f32[8]{0:T(128)} %param.19) | copy-start | bytes 100
  45.7 6.0 %copy-start.17 = (f32[8]{0:T(128)S(1)}, f32[8]{0:T(128)}, u32[]{:S(2)}) copy-start(f32[8]{0:T(128)} %param.18) | copy-start | bytes 100
  45.7 13.0 %copy-start.4 = (f32[1,2,256,128]{3,2,1,0:T(8,128)S(1)}, f32[1,2,256,128]{3,2,1,0:T(8,128)}, u32[]{:S(2)}) copy-start(f32[1,2,256,128]{3,2,1,0:T(8,128)} %get-tuple-element.61) | copy-start | bytes 786436
  45.7 13.0 %copy-start.11 = (s32[2,256,128]{2,1,0:T(8,128)S(1)}, s32[2,256,128]{2,1,0:T(8,128)}, u32[]{:S(2)}) copy-start(s32[2,256,128]{2,1,0:T(8,128)} %param.17) | copy-start | bytes 786436
  46.7 5.7 %collective-permute-start.4 = (f32[1,128,256]{2,1,0:T(8,128)S(1)}, f32[1,128,256]{2,1,0:T(8,128)S(1)}, u32[]{:S(2)}, u32[]{:S(2)}) collective-permute-start(f32[1,128,256]{2,1,0:T(8,128)S(1)} %get-tuple-element.87), channel_id=1, source_target_pairs={{2,0},{4,2},{6,4},{8,6},{10,8},{12,10},{14,12},{16,14},{18,16},{20... | collective-permute-start | bytes 393224 | tf_op jit(solution)/shard_map/ppermute | solution.py:21
  48.6 7.2 %collective-permute-start.5 = (f32[1,128,256]{2,1,0:T(8,128)S(1)}, f32[1,128,256]{2,1,0:T(8,128)S(1)}, u32[]{:S(2)}, u32[]{:S(2)}) collective-permute-start(f32[1,128,256]{2,1,0:T(8,128)S(1)} %get-tuple-element.86), channel_id=1, source_target_pairs={{0,2},{2,4},{4,6},{6,8},{8,10},{10,12},{12,14},{14,16},{16,18},{18... | collective-permute-start | bytes 393224 | tf_op jit(solution)/shard_map/ppermute | solution.py:20
  55.8 14.5 %collective-permute-start.6 = (f32[4,1,256]{2,1,0:T(1,128)S(1)}, f32[4,1,256]{2,1,0:T(1,128)S(1)}, u32[]{:S(2)}, u32[]{:S(2)}) collective-permute-start(f32[4,1,256]{2,1,0:T(1,128)S(1)} %get-tuple-element.83), channel_id=1, source_target_pairs={{1,0},{3,2},{5,4},{7,6},{9,8},{11,10},{13,12},{15,14},{17,16},{19,... | collective-permute-start | bytes 12296 | tf_op jit(solution)/shard_map/ppermute | solution.py:21
  57.4 12.8 %collective-permute-start.7 = (f32[4,1,256]{2,1,0:T(1,128)S(1)}, f32[4,1,256]{2,1,0:T(1,128)S(1)}, u32[]{:S(2)}, u32[]{:S(2)}) collective-permute-start(f32[4,1,256]{2,1,0:T(1,128)S(1)} %get-tuple-element.82), channel_id=1, source_target_pairs={{0,1},{2,3},{4,5},{6,7},{8,9},{10,11},{12,13},{14,15},{16,17},{18,... | collective-permute-start | bytes 12296 | tf_op jit(solution)/shard_map/ppermute | solution.py:20
  70.6 8.6 %copy-start.5 = (f32[1,2,256,128]{3,2,1,0:T(8,128)S(1)}, f32[1,2,256,128]{3,2,1,0:T(8,128)}, u32[]{:S(2)}) copy-start(f32[1,2,256,128]{3,2,1,0:T(8,128)} %get-tuple-element.61) | copy-start | bytes 786436
  70.6 8.6 %copy-start.8 = (f32[2,256,128]{2,1,0:T(8,128)S(1)}, f32[2,256,128]{2,1,0:T(8,128)}, u32[]{:S(2)}) copy-start(f32[2,256,128]{2,1,0:T(8,128)} %get-tuple-element.51) | copy-start | bytes 786436
  70.6 8.6 %copy-start.12 = (pred[2,256,128]{2,1,0:T(8,128)(4,1)S(1)}, pred[2,256,128]{2,1,0:T(8,128)(4,1)}, u32[]{:S(2)}) copy-start(pred[2,256,128]{2,1,0:T(8,128)(4,1)} %get-tuple-element.54) | copy-start | bytes 196612
  70.6 8.6 %copy-start.13 = (pred[2,256,128]{2,1,0:T(8,128)(4,1)S(1)}, pred[2,256,128]{2,1,0:T(8,128)(4,1)}, u32[]{:S(2)}) copy-start(pred[2,256,128]{2,1,0:T(8,128)(4,1)} %get-tuple-element.55) | copy-start | bytes 196612
  70.6 8.6 %copy-start.14 = (pred[2,256,128]{2,1,0:T(8,128)(4,1)S(1)}, pred[2,256,128]{2,1,0:T(8,128)(4,1)}, u32[]{:S(2)}) copy-start(pred[2,256,128]{2,1,0:T(8,128)(4,1)} %get-tuple-element.56) | copy-start | bytes 196612
  70.7 8.6 %copy-start.15 = (pred[2,256,128]{2,1,0:T(8,128)(4,1)S(1)}, pred[2,256,128]{2,1,0:T(8,128)(4,1)}, u32[]{:S(2)}) copy-start(pred[2,256,128]{2,1,0:T(8,128)(4,1)} %get-tuple-element.57) | copy-start | bytes 196612
  71.5 0.7 copy-start.10
  73.0 17.7 %copy-start.3 = (f32[2,256,128]{2,1,0:T(8,128)S(1)}, f32[2,256,128]{2,1,0:T(8,128)}, u32[]{:S(2)}) copy-start(f32[2,256,128]{2,1,0:T(8,128)} %copy-done.2) | copy-start | bytes 786436
  73.0 17.7 %copy-start.7 = (f32[2,256,128]{2,1,0:T(8,128)S(1)}, f32[2,256,128]{2,1,0:T(8,128)}, u32[]{:S(2)}) copy-start(f32[2,256,128]{2,1,0:T(8,128)} %get-tuple-element.50) | copy-start | bytes 786436
  73.0 17.4 %all-to-all-start.1 = ((f32[2,128,256]{1,0,2:T(2,128)}), f32[2,128,256]{1,0,2:T(2,128)S(1)}, u32[]{:S(2)}, u32[]{:S(2)}) async-start(f32[2,128,256]{1,0,2:T(2,128)} %copy.256), calls=%async_computation.1 | async-start | bytes 524288 | tf_op jit(solution)/shard_map/all_to_all | solution.py:151
  94.2 5.6 %collective-permute-start.8 = (f32[3,3,256]{2,1,0:T(4,128)S(1)}, f32[3,3,256]{2,1,0:T(4,128)S(1)}, u32[]{:S(2)}, u32[]{:S(2)}) collective-permute-start(f32[3,3,256]{2,1,0:T(4,128)S(1)} %slice_reduce_fusion), channel_id=1, source_target_pairs={{0,1},{2,3},{4,5},{6,7},{8,9},{10,11},{12,13},{14,15},{16,17},{18,... | collective-permute-start | bytes 27656 | tf_op jit(solution)/shard_map/ppermute | solution.py:29
  107.8 10.0 %collective-permute-start.9 = (f32[3,256,128]{2,1,0:T(8,128)S(1)}, f32[3,256,128]{2,1,0:T(8,128)S(1)}, u32[]{:S(2)}, u32[]{:S(2)}) collective-permute-start(f32[3,256,128]{2,1,0:T(8,128)S(1)} %slice_bitcast_fusion.2), channel_id=1, source_target_pairs={{0,2},{2,4},{4,6},{6,8},{8,10},{10,12},{12,14},{14,16},{16,18},{18... | collective-permute-start | bytes 1179656 | tf_op jit(solution)/shard_map/ppermute | solution.py:29
where the time goes:
time: 120 us; the launch traced here: 119 us
  other arithmetic  48.5 us (40%)
  starting transfers between devices  33.7 us (28%)
  local copies, waits for them, and re-layouts  20.2 us (17%)
  waiting for transfers between devices  15.3 us (13%)
    another operation x2, other arithmetic, on_device(): jnp.stack([pressure, conduct])  13.9 us
    ppermute x4, starting transfers between devices, extended(): after = lax.ppermute(leading, axis, down)  12.6 us
    ppermute x2, waiting for transfers between devices, passed_along(): return lax.ppermute(block, axis, route)  11.9 us
    max x1, other arithmetic, plastic(): jnp.maximum(1.0 - SHEAR * multiplier / jnp.maximum(equiv_shear, FLOOR), 0.0)  11.5 us
    div x1, other arithmetic, plastic(): return deviator * shrink_factor + normal_mask * (new_invariant / 3.0)  11.2 us
    scatter-add x1, local copies, waits for them, and re-layouts, on_device(): node_main = node_main.at[:, :, :, 0].add(from_below)  7.48 us
    ppermute x4, starting transfers between devices, extended(): before = lax.ppermute(last, axis, up)  7.03 us
    all_to_all x1, starting transfers between devices, on_device(): lax.all_to_all(pressure_next, 'gz', split_axis=2, concat_axis=1, tiled=True)  6.2 us
  transfers between devices with their start and end apart: 12, of which 3 were waited for; matrix products, arithmetic and copies ran while one was open for 28% of the time, Pallas kernels for 0%

commit v1 on v0

--- a/solution.py
+++ b/solution.py
@@ -148,7 +148,10 @@
     bordered = extended(first_sweep, (("gx", 0), ("gz", 1)), 1)
     bordered = jnp.pad(bordered, ((0, 0), (0, 0), (1, 1)))
     pressure_next = relax_padded(bordered, pressure_pair[1], storage, source)
-    pressure_block = lax.all_to_all(pressure_next, "gz", split_axis=2, concat_axis=1, tiled=True)
+    peers = lax.axis_size("gz")
+    parts = jnp.stack(jnp.split(pressure_next, peers, axis=2), axis=0)
+    parts = lax.all_to_all(parts, "gz", split_axis=0, concat_axis=0)
+    pressure_block = jnp.concatenate(parts, axis=1)
     col_x, col_y, col_z = corner_terms(stress_next, pressure_block)
     node_main, node_rim = node_parts(col_x, col_y, col_z)
     from_below = passed_along(node_rim, "gz", 1)

time: 120 us -> 120 us (level)
    unnamed x38 -> x42, local copies, waits for them, and re-layouts: 2.45 us -> 3.23 us
where the time goes in v1:
time: 120 us; the launch traced here: 118 us
  other arithmetic  48.5 us (40%)
  starting transfers between devices  33.6 us (28%)
  local copies, waits for them, and re-layouts  20 us (17%)
  waiting for transfers between devices  15.3 us (13%)
    another operation x2, other arithmetic, on_device(): jnp.stack([pressure, conduct])  13.2 us
    ppermute x4, starting transfers between devices, extended(): after = lax.ppermute(leading, axis, down)  12.7 us
    ppermute x2, waiting for transfers between devices, passed_along(): return lax.ppermute(block, axis, route)  11.9 us
    max x1, other arithmetic, plastic(): jnp.maximum(1.0 - SHEAR * multiplier / jnp.maximum(equiv_shear, FLOOR), 0.0)  11.6 us
    div x1, other arithmetic, plastic(): return deviator * shrink_factor + normal_mask * (new_invariant / 3.0)  11.3 us
    scatter-add x1, local copies, waits for them, and re-layouts, on_device(): node_main = node_main.at[:, :, :, 0].add(from_below)  7.48 us
    ppermute x4, starting transfers between devices, extended(): before = lax.ppermute(last, axis, up)  7.03 us
    all_to_all x1, starting transfers between devices, on_device(): parts = lax.all_to_all(parts, 'gz', split_axis=0, concat_axis=0)  6.07 us
  transfers between devices with their start and end apart: 12, of which 3 were waited for; matrix products, arithmetic and copies ran while one was open for 28% of the time, Pallas kernels for 0%

profile of v1, /device:TPU:10, one launch (start us, length us, event | category | flops | bytes accessed | tf_op | source)
XLA Modules:
  0.0 118.5 jit_solution(4508041559652973038)
XLA Ops:
  0.6 2.0 %fusion.46 = (f32[1]{0:T(128)}, f32[1]{0:T(128)}, f32[1]{0:T(128)}, f32[1]{0:T(128)}, f32[1]{0:T(128)}, /*index=5*/f32[1]{0:T(128)}, f32[1]{0:T(128)}, f32[1]{0:...) fusion(f32[16]{0:T(128)} %param.23), kind=kLoop, calls=%fused_computation.151 | loop fusion | bytes 128 | tf_op jit(solution)/shard_map/slice | solution.py:35
  2.6 11.4 %add_bitcast_fusion = f32[1,2,128,256]{3,2,1,0:T(8,128)S(1)} fusion(s32[2,128,256]{2,1,0:T(8,128)} %param.22, f32[]{:T(128)} %bitcast.19, f32[]{:T(128)} %bitcast.18, f32[]{:T(128)} %bitcast.17, f32[]{:T(128)} %bitcast.16, f32[]{:T(128)} %bitcast.15, f32[]{:T(128)} %bitcast.14, f32[]{:T(128)} %bitcast.13, f32[]{:T(128)} %bitcast.12, f32[]{:T(128)} %bitcast.11, ...), kind=kLoop, calls=%fused_computation.126 | loop fusion | flops 3080192 | bytes 524352 | tf_op jit(solution)/shard_map/stack | solution.py:145
  14.0 0.0 copy-start.1
  14.0 0.7 copy-done.1
  14.7 1.8 %fusion.11 = (f32[2,1,128,256]{3,2,1,0:T(8,128)}, f32[2,1,128,256]{3,2,1,0:T(8,128)}) fusion(f32[1,2,128,256]{3,2,1,0:T(8,128)} %bitcast.81, f32[1,2,128,256]{3,2,1,0:T(8,128)S(1)} %add_bitcast_fusion), kind=kLoop, calls=%fused_computation.57 | loop fusion | flops 131072 | bytes 1048576 | tf_op jit(solution)/shard_map/stack | solution.py:145
  16.5 2.0 %collective-permute-start = (f32[2,1,128,256]{3,2,1,0:T(8,128)}, f32[2,1,128,256]{3,2,1,0:T(8,128)}, u32[]{:S(2)}, u32[]{:S(2)}) collective-permute-start(f32[2,1,128,256]{3,2,1,0:T(8,128)} %get-tuple-element.81), channel_id=1, source_target_pairs={{0,2},{2,4},{4,6},{6,8},{8,10},{10,12},{12,14},{14,16},{16,18},{18... | collective-permute-start | bytes 786440 | tf_op jit(solution)/shard_map/ppermute | solution.py:20
  18.5 4.5 %collective-permute-start.1 = (f32[2,1,128,256]{3,2,1,0:T(8,128)}, f32[2,1,128,256]{3,2,1,0:T(8,128)}, u32[]{:S(2)}, u32[]{:S(2)}) collective-permute-start(f32[2,1,128,256]{3,2,1,0:T(8,128)} %get-tuple-element.82), channel_id=1, source_target_pairs={{2,0},{4,2},{6,4},{8,6},{10,8},{12,10},{14,12},{16,14},{18,16},{20... | collective-permute-start | bytes 786440 | tf_op jit(solution)/shard_map/ppermute | solution.py:21
  23.2 0.9 copy.157
  24.1 4.6 %all-to-all-start = ((f32[2,256,128]{2,0,1:T(2,128)}), f32[2,256,128]{2,0,1:T(2,128)}, u32[]{:S(2)}, u32[]{:S(2)}) async-start(f32[2,256,128]{2,0,1:T(2,128)} %copy.157), calls=%async_computation | async-start | bytes 524288 | tf_op jit(solution)/shard_map/all_to_all | solution.py:141
  28.7 1.8 %multiply_add_fusion.1 = f32[6,2,256,128]{3,2,1,0:T(8,128)S(1)} fusion(f32[6,2,256,128]{3,2,1,0:T(8,128)} %param.16, f32[6,2,256,128]{3,2,1,0:T(8,128)S(1)} %copy-done.3, f32[2,256,128]{2,1,0:T(8,128)S(1)} %multiply_bitcast_fusion.1, f32[2,256,128]{2,1,0:T(8,128)S(1)} %get-tuple-element.59, f32[6]{0:T(128)S(1)} %copy-done.20), kind=kLoop, calls=%fused_computation.11 | loop fusion | flops 2359296 | bytes 5242904 | tf_op jit(solution)/shard_map/add | solution.py:68
  30.5 0.8 multiply_bitcast_fusion
  31.3 0.2 multiply_subtract_fusion.1
  31.5 0.5 copy-done.4
  32.0 0.0 collective-permute-done
  32.0 0.0 collective-permute-done.1
  32.0 0.3 copy-done
  32.3 0.1 copy-done.2
  32.4 0.8 pad_maximum_fusion.16
  33.2 1.3 %collective-permute-start.2 = (f32[2,4,1,256]{3,2,1,0:T(1,128)S(1)}, f32[2,4,1,256]{3,2,1,0:T(1,128)S(1)}, u32[]{:S(2)}, u32[]{:S(2)}) collective-permute-start(f32[2,4,1,256]{3,2,1,0:T(1,128)S(1)} %get-tuple-element.77), channel_id=1, source_target_pairs={{0,1},{2,3},{4,5},{6,7},{8,9},{10,11},{12,13},{14,15},{16,17},{18,... | collective-permute-start | bytes 24584 | tf_op jit(solution)/shard_map/ppermute | solution.py:20
  34.5 4.5 %collective-permute-start.3 = (f32[2,4,1,256]{3,2,1,0:T(1,128)S(1)}, f32[2,4,1,256]{3,2,1,0:T(1,128)S(1)}, u32[]{:S(2)}, u32[]{:S(2)}) collective-permute-start(f32[2,4,1,256]{3,2,1,0:T(1,128)S(1)} %get-tuple-element.78), channel_id=1, source_target_pairs={{1,0},{3,2},{5,4},{7,6},{9,8},{11,10},{13,12},{15,14},{17,16},{19,... | collective-permute-start | bytes 24584 | tf_op jit(solution)/shard_map/ppermute | solution.py:21
  39.1 1.1 broadcast_multiply_fusion
  40.1 0.9 copy.158
  41.0 1.9 %mul.293 = f32[2,128,256]{2,1,0:T(8,128)} reshape(f32[2,128,2,128]{3,2,1,0:T(2,128)} %copy.158) | data formatting | bytes 524288 | tf_op jit(solution)/shard_map/mul | solution.py:144
  42.9 1.7 %select_maximum_fusion = f32[2,4,130,258]{3,2,1,0:T(8,128)S(1)} fusion(f32[2,4,1,256]{3,2,1,0:T(1,128)S(1)} %collective-permute-done.3, f32[2,4,1,256]{3,2,1,0:T(1,128)S(1)} %collective-permute-done.2, f32[2,1,128,256]{3,2,1,0:T(8,128)} %collective-permute-done.1, f32[2,1,128,256]{3,2,1,0:T(8,128)} %collective-permute-done, f32[1,2,128,256]{3,2,1,0:T(8,128)} %copy-done.1, ...), kind=kLoop, calls=%fused_computation.2 | loop fusion | flops 3756480 | bytes 2138240 | tf_op jit(solution)/shard_map/concatenate | solution.py:22
  44.6 0.0 copy-start.8
  44.6 0.0 copy-start.11
  44.6 0.1 slice_bitcast_fusion.1
  44.8 0.8 copy-done.8
  45.6 0.1 copy-done.11
  45.7 0.9 fusion.32
  46.6 1.9 %collective-permute-start.4 = (f32[1,128,256]{2,1,0:T(8,128)S(1)}, f32[1,128,256]{2,1,0:T(8,128)S(1)}, u32[]{:S(2)}, u32[]{:S(2)}) collective-permute-start(f32[1,128,256]{2,1,0:T(8,128)S(1)} %get-tuple-element.86), channel_id=1, source_target_pairs={{2,0},{4,2},{6,4},{8,6},{10,8},{12,10},{14,12},{16,14},{18,16},{20... | collective-permute-start | bytes 393224 | tf_op jit(solution)/shard_map/ppermute | solution.py:21
  48.5 2.4 %collective-permute-start.5 = (f32[1,128,256]{2,1,0:T(8,128)S(1)}, f32[1,128,256]{2,1,0:T(8,128)S(1)}, u32[]{:S(2)}, u32[]{:S(2)}) collective-permute-start(f32[1,128,256]{2,1,0:T(8,128)S(1)} %get-tuple-element.85), channel_id=1, source_target_pairs={{0,2},{2,4},{4,6},{6,8},{8,10},{10,12},{12,14},{14,16},{16,18},{18... | collective-permute-start | bytes 393224 | tf_op jit(solution)/shard_map/ppermute | solution.py:20
  51.0 0.7 fusion.44
  51.6 0.7 fusion.45
  52.3 3.4 %collective-permute-done.5 = f32[1,128,256]{2,1,0:T(8,128)S(1)} collective-permute-done((f32[1,128,256]{2,1,0:T(8,128)S(1)}, f32[1,128,256]{2,1,0:T(8,128)S(1)}, u32[]{:S(2)}, u32[]{:S(2)}) %collective-permute-start.5) | collective-permute-done | bytes 131104 | tf_op jit(solution)/shard_map/ppermute | solution.py:20
  55.7 1.7 %collective-permute-start.6 = (f32[4,1,256]{2,1,0:T(1,128)S(1)}, f32[4,1,256]{2,1,0:T(1,128)S(1)}, u32[]{:S(2)}, u32[]{:S(2)}) collective-permute-start(f32[4,1,256]{2,1,0:T(1,128)S(1)} %get-tuple-element.80), channel_id=1, source_target_pairs={{1,0},{3,2},{5,4},{7,6},{9,8},{11,10},{13,12},{15,14},{17,16},{19,... | collective-permute-start | bytes 12296 | tf_op jit(solution)/shard_map/ppermute | solution.py:21
  57.4 1.3 %collective-permute-start.7 = (f32[4,1,256]{2,1,0:T(1,128)S(1)}, f32[4,1,256]{2,1,0:T(1,128)S(1)}, u32[]{:S(2)}, u32[]{:S(2)}) collective-permute-start(f32[4,1,256]{2,1,0:T(1,128)S(1)} %get-tuple-element.79), channel_id=1, source_target_pairs={{0,1},{2,3},{4,5},{6,7},{8,9},{10,11},{12,13},{14,15},{16,17},{18,... | collective-permute-start | bytes 12296 | tf_op jit(solution)/shard_map/ppermute | solution.py:20
  58.7 11.6 %subtract_maximum_fusion = (f32[2,256,128]{2,1,0:T(8,128)}, f32[2,256,128]{2,1,0:T(8,128)}, pred[2,256,128]{2,1,0:T(8,128)(4,1)S(1)}, pred[2,256,128]{2,1,0:T(8,...) fusion(f32[]{:T(128)} %bitcast.43, f32[]{:T(128)} %bitcast.42, ...), kind=kLoop, calls=%fused_computation.115 | loop fusion | flops 4063232 | bytes 3145792 | tf_op jit(solution)/shard_map/max | solution.py:88
  70.3 0.3 select_maximum_fusion.5
  70.6 0.8 fusion.21
  71.4 0.0 copy-start.12
  71.4 0.7 copy-done.12
  72.2 0.0 copy-start.9
  72.2 0.7 pad_maximum_fusion.12
  72.9 6.1 %all-to-all-start.1 = ((f32[2,2,128,128]{3,2,1,0:T(8,128)}), f32[2,2,128,128]{3,2,1,0:T(8,128)S(1)}, u32[]{:S(2)}, u32[]{:S(2)}) async-start(f32[2,2,128,128]{3,2,1,0:T(8,128)} %pad_maximum_fusion.12), calls=%async_computation.1 | async-start | bytes 524288 | tf_op jit(solution)/shard_map/all_to_all | solution.py:153
  79.0 11.3 %fusion.10 = f32[2,256,128]{2,1,0:T(8,128)S(1)} fusion(f32[1,2,256,128]{3,2,1,0:T(8,128)S(1)} %copy-done.7, pred[2,256,128]{2,1,0:T(8,128)(4,1)} %get-tuple-element.56, f32[]{:T(128)} %bitcast.43, pred[2,256,128]{2,1,0:T(8,128)(4,1)} %get-tuple-element.55, f32[]{:T(128)} %bitcast.42, pred[2,256,128]{2,1,0:T(8,128)(4,1)S(1)} %copy-done.17, f32[]{:T(128)} %bitcast.41, ...), kind=kLoop, calls=%fused_computation.56 | loop fusion | flops 2686976 | bytes 1310784 | tf_op jit(solution)/shard_map/div | solution.py:90
  90.4 1.6 %multiply_subtract_fusion = (f32[6,2,256,128]{3,2,1,0:T(8,128)S(1)}, f32[6,2,256,128]{3,2,1,0:T(8,128)}) fusion(f32[2,256,128]{2,1,0:T(8,128)S(1)} %bitcast.85, f32[6]{0:T(128)S(1)} %copy-done.20, f32[2,256,128]{2,1,0:T(8,128)S(1)} %fusion.10, f32[2,256,128]{2,1,0:T(8,128)S(1)} %copy-done.9, f32[6,2,256,128]{3,2,1,0:T(8,128)S(1)} %multiply_add_fusion.1, ...), kind=kLoop, calls=%fused_computation.8 | loop fusion | flops 2752512 | bytes 5767192 | tf_op jit(solution)/shard_map/sub | solution.py:95
  92.0 0.1 fusion.42
  92.1 0.2 add_multiply_fusion.7
  92.3 0.2 add_multiply_fusion.6
  92.4 0.2 add_multiply_fusion
  92.6 0.2 add_multiply_fusion.4
  92.9 0.2 fusion.5
  93.1 0.7 slice_reduce_fusion
  93.8 1.3 %collective-permute-start.8 = (f32[3,3,256]{2,1,0:T(4,128)S(1)}, f32[3,3,256]{2,1,0:T(4,128)S(1)}, u32[]{:S(2)}, u32[]{:S(2)}) collective-permute-start(f32[3,3,256]{2,1,0:T(4,128)S(1)} %slice_reduce_fusion), channel_id=1, source_target_pairs={{0,1},{2,3},{4,5},{6,7},{8,9},{10,11},{12,13},{14,15},{16,17},{18,... | collective-permute-start | bytes 27656 | tf_op jit(solution)/shard_map/ppermute | solution.py:29
  95.1 0.5 fusion.3
  95.6 3.8 %collective-permute-done.8 = f32[3,3,256]{2,1,0:T(4,128)S(1)} collective-permute-done((f32[3,3,256]{2,1,0:T(4,128)S(1)}, f32[3,3,256]{2,1,0:T(4,128)S(1)}, u32[]{:S(2)}, u32[]{:S(2)}) %collective-permute-start.8) | collective-permute-done | bytes 9248 | tf_op jit(solution)/shard_map/ppermute | solution.py:29
  99.4 0.4 copy.160
  99.8 0.1 slice_add_fusion
  99.9 7.5 %scatter-add.6 = f32[3,3,256,128]{3,2,1,0:T(8,128)S(1)} dynamic-update-slice(f32[3,3,256,128]{3,2,1,0:T(8,128)S(1)} %fusion.3, f32[3,3,256,1]{3,2,1,0:T(8,128)S(1)} %slice_add_fusion, s32[]{:T(128)} %constant.100.clone.1, s32[]{:T(128)} %constant.100.clone.1, s32[]{:T(128)} %constant.100.clone.1, s32[]{:T(128)} %constant.100.clone.1) | dynamic-update-slice | bytes 18436 | tf_op jit(solution)/shard_map/scatter-add | solution.py:158
  107.4 1.9 %collective-permute-start.9 = (f32[3,256,128]{2,1,0:T(8,128)S(1)}, f32[3,256,128]{2,1,0:T(8,128)S(1)}, u32[]{:S(2)}, u32[]{:S(2)}) collective-permute-start(f32[3,256,128]{2,1,0:T(8,128)S(1)} %slice_bitcast_fusion.2), channel_id=1, source_target_pairs={{0,2},{2,4},{4,6},{6,8},{8,10},{10,12},{12,14},{14,16},{16,18},{18... | collective-permute-start | bytes 1179656 | tf_op jit(solution)/shard_map/ppermute | solution.py:29
  109.4 8.1 %collective-permute-done.9 = f32[3,256,128]{2,1,0:T(8,128)S(1)} collective-permute-done((f32[3,256,128]{2,1,0:T(8,128)S(1)}, f32[3,256,128]{2,1,0:T(8,128)S(1)}, u32[]{:S(2)}, u32[]{:S(2)}) %collective-permute-start.9) | collective-permute-done | bytes 393248 | tf_op jit(solution)/shard_map/ppermute | solution.py:29
  117.4 0.1 fusion.7
  117.5 0.9 slice.475
  (44 shorter events, 0.2 us)
Async XLA Ops:
  0.6 22.5 %copy-start.3 = (f32[6,2,256,128]{3,2,1,0:T(8,128)S(1)}, f32[6,2,256,128]{3,2,1,0:T(8,128)}, u32[]{:S(2)}) copy-start(f32[6,2,256,128]{3,2,1,0:T(8,128)} %param.15) | copy-start | bytes 4718596
  14.0 0.7 copy-start.1
  16.5 12.2 %copy-start.20 = (f32[6]{0:T(128)S(1)}, f32[6]{0:T(128)}, u32[]{:S(2)}) copy-start(f32[6]{0:T(128)} %constant.126.clone) | copy-start | bytes 76
  16.5 15.5 %collective-permute-start = (f32[2,1,128,256]{3,2,1,0:T(8,128)}, f32[2,1,128,256]{3,2,1,0:T(8,128)}, u32[]{:S(2)}, u32[]{:S(2)}) collective-permute-start(f32[2,1,128,256]{3,2,1,0:T(8,128)} %get-tuple-element.81), channel_id=1, source_target_pairs={{0,2},{2,4},{4,6},{6,8},{8,10},{10,12},{12,14},{14,16},{16,18},{18... | collective-permute-start | bytes 786440 | tf_op jit(solution)/shard_map/ppermute | solution.py:20
  18.5 13.4 %collective-permute-start.1 = (f32[2,1,128,256]{3,2,1,0:T(8,128)}, f32[2,1,128,256]{3,2,1,0:T(8,128)}, u32[]{:S(2)}, u32[]{:S(2)}) collective-permute-start(f32[2,1,128,256]{3,2,1,0:T(8,128)} %get-tuple-element.82), channel_id=1, source_target_pairs={{2,0},{4,2},{6,4},{8,6},{10,8},{12,10},{14,12},{16,14},{18,16},{20... | collective-permute-start | bytes 786440 | tf_op jit(solution)/shard_map/ppermute | solution.py:21
  24.1 15.0 %all-to-all-start = ((f32[2,256,128]{2,0,1:T(2,128)}), f32[2,256,128]{2,0,1:T(2,128)}, u32[]{:S(2)}, u32[]{:S(2)}) async-start(f32[2,256,128]{2,0,1:T(2,128)} %copy.157), calls=%async_computation | async-start | bytes 524288 | tf_op jit(solution)/shard_map/all_to_all | solution.py:141
  31.3 0.7 copy-start.4
  31.3 1.0 copy-start
  31.3 1.1 copy-start.2
  33.2 9.7 %collective-permute-start.2 = (f32[2,4,1,256]{3,2,1,0:T(1,128)S(1)}, f32[2,4,1,256]{3,2,1,0:T(1,128)S(1)}, u32[]{:S(2)}, u32[]{:S(2)}) collective-permute-start(f32[2,4,1,256]{3,2,1,0:T(1,128)S(1)} %get-tuple-element.77), channel_id=1, source_target_pairs={{0,1},{2,3},{4,5},{6,7},{8,9},{10,11},{12,13},{14,15},{16,17},{18,... | collective-permute-start | bytes 24584 | tf_op jit(solution)/shard_map/ppermute | solution.py:20
  34.5 8.4 %collective-permute-start.3 = (f32[2,4,1,256]{3,2,1,0:T(1,128)S(1)}, f32[2,4,1,256]{3,2,1,0:T(1,128)S(1)}, u32[]{:S(2)}, u32[]{:S(2)}) collective-permute-start(f32[2,4,1,256]{3,2,1,0:T(1,128)S(1)} %get-tuple-element.78), channel_id=1, source_target_pairs={{1,0},{3,2},{5,4},{7,6},{9,8},{11,10},{13,12},{15,14},{17,16},{19,... | collective-permute-start | bytes 24584 | tf_op jit(solution)/shard_map/ppermute | solution.py:21
  44.6 1.0 copy-start.8
  44.6 1.0 copy-start.11
  45.7 5.3 %copy-start.18 = (f32[8]{0:T(128)S(1)}, f32[8]{0:T(128)}, u32[]{:S(2)}) copy-start(f32[8]{0:T(128)} %param.19) | copy-start | bytes 100
  45.7 6.0 %copy-start.19 = (f32[8]{0:T(128)S(1)}, f32[8]{0:T(128)}, u32[]{:S(2)}) copy-start(f32[8]{0:T(128)} %param.18) | copy-start | bytes 100
  45.7 13.1 %copy-start.6 = (f32[1,2,256,128]{3,2,1,0:T(8,128)S(1)}, f32[1,2,256,128]{3,2,1,0:T(8,128)}, u32[]{:S(2)}) copy-start(f32[1,2,256,128]{3,2,1,0:T(8,128)} %get-tuple-element.58) | copy-start | bytes 786436
  45.7 13.1 %copy-start.13 = (s32[2,256,128]{2,1,0:T(8,128)S(1)}, s32[2,256,128]{2,1,0:T(8,128)}, u32[]{:S(2)}) copy-start(s32[2,256,128]{2,1,0:T(8,128)} %param.17) | copy-start | bytes 786436
  46.6 5.7 %collective-permute-start.4 = (f32[1,128,256]{2,1,0:T(8,128)S(1)}, f32[1,128,256]{2,1,0:T(8,128)S(1)}, u32[]{:S(2)}, u32[]{:S(2)}) collective-permute-start(f32[1,128,256]{2,1,0:T(8,128)S(1)} %get-tuple-element.86), channel_id=1, source_target_pairs={{2,0},{4,2},{6,4},{8,6},{10,8},{12,10},{14,12},{16,14},{18,16},{20... | collective-permute-start | bytes 393224 | tf_op jit(solution)/shard_map/ppermute | solution.py:21
  48.5 7.2 %collective-permute-start.5 = (f32[1,128,256]{2,1,0:T(8,128)S(1)}, f32[1,128,256]{2,1,0:T(8,128)S(1)}, u32[]{:S(2)}, u32[]{:S(2)}) collective-permute-start(f32[1,128,256]{2,1,0:T(8,128)S(1)} %get-tuple-element.85), channel_id=1, source_target_pairs={{0,2},{2,4},{4,6},{6,8},{8,10},{10,12},{12,14},{14,16},{16,18},{18... | collective-permute-start | bytes 393224 | tf_op jit(solution)/shard_map/ppermute | solution.py:20
  55.7 14.6 %collective-permute-start.6 = (f32[4,1,256]{2,1,0:T(1,128)S(1)}, f32[4,1,256]{2,1,0:T(1,128)S(1)}, u32[]{:S(2)}, u32[]{:S(2)}) collective-permute-start(f32[4,1,256]{2,1,0:T(1,128)S(1)} %get-tuple-element.80), channel_id=1, source_target_pairs={{1,0},{3,2},{5,4},{7,6},{9,8},{11,10},{13,12},{15,14},{17,16},{19,... | collective-permute-start | bytes 12296 | tf_op jit(solution)/shard_map/ppermute | solution.py:21
  57.4 12.9 %collective-permute-start.7 = (f32[4,1,256]{2,1,0:T(1,128)S(1)}, f32[4,1,256]{2,1,0:T(1,128)S(1)}, u32[]{:S(2)}, u32[]{:S(2)}) collective-permute-start(f32[4,1,256]{2,1,0:T(1,128)S(1)} %get-tuple-element.79), channel_id=1, source_target_pairs={{0,1},{2,3},{4,5},{6,7},{8,9},{10,11},{12,13},{14,15},{16,17},{18,... | collective-permute-start | bytes 12296 | tf_op jit(solution)/shard_map/ppermute | solution.py:20
  71.4 0.7 copy-start.12
  72.1 6.9 %copy-start.7 = (f32[1,2,256,128]{3,2,1,0:T(8,128)S(1)}, f32[1,2,256,128]{3,2,1,0:T(8,128)}, u32[]{:S(2)}) copy-start(f32[1,2,256,128]{3,2,1,0:T(8,128)} %get-tuple-element.58) | copy-start | bytes 786436
  72.1 6.9 %copy-start.10 = (f32[2,256,128]{2,1,0:T(8,128)S(1)}, f32[2,256,128]{2,1,0:T(8,128)}, u32[]{:S(2)}) copy-start(f32[2,256,128]{2,1,0:T(8,128)} %get-tuple-element.48) | copy-start | bytes 786436
  72.1 6.9 %copy-start.14 = (pred[2,256,128]{2,1,0:T(8,128)(4,1)S(1)}, pred[2,256,128]{2,1,0:T(8,128)(4,1)}, u32[]{:S(2)}) copy-start(pred[2,256,128]{2,1,0:T(8,128)(4,1)} %get-tuple-element.51) | copy-start | bytes 196612
  72.1 6.9 %copy-start.15 = (pred[2,256,128]{2,1,0:T(8,128)(4,1)S(1)}, pred[2,256,128]{2,1,0:T(8,128)(4,1)}, u32[]{:S(2)}) copy-start(pred[2,256,128]{2,1,0:T(8,128)(4,1)} %get-tuple-element.52) | copy-start | bytes 196612
  72.2 6.9 %copy-start.16 = (pred[2,256,128]{2,1,0:T(8,128)(4,1)S(1)}, pred[2,256,128]{2,1,0:T(8,128)(4,1)}, u32[]{:S(2)}) copy-start(pred[2,256,128]{2,1,0:T(8,128)(4,1)} %get-tuple-element.53) | copy-start | bytes 196612
  72.2 6.9 %copy-start.17 = (pred[2,256,128]{2,1,0:T(8,128)(4,1)S(1)}, pred[2,256,128]{2,1,0:T(8,128)(4,1)}, u32[]{:S(2)}) copy-start(pred[2,256,128]{2,1,0:T(8,128)(4,1)} %get-tuple-element.54) | copy-start | bytes 196612
  72.2 18.1 %copy-start.5 = (f32[2,256,128]{2,1,0:T(8,128)S(1)}, f32[2,256,128]{2,1,0:T(8,128)}, u32[]{:S(2)}) copy-start(f32[2,256,128]{2,1,0:T(8,128)} %copy-done.4) | copy-start | bytes 786436
  72.2 18.1 %copy-start.9 = (f32[2,256,128]{2,1,0:T(8,128)S(1)}, f32[2,256,128]{2,1,0:T(8,128)}, u32[]{:S(2)}) copy-start(f32[2,256,128]{2,1,0:T(8,128)} %get-tuple-element.47) | copy-start | bytes 786436
  72.9 17.4 %all-to-all-start.1 = ((f32[2,2,128,128]{3,2,1,0:T(8,128)}), f32[2,2,128,128]{3,2,1,0:T(8,128)S(1)}, u32[]{:S(2)}, u32[]{:S(2)}) async-start(f32[2,2,128,128]{3,2,1,0:T(8,128)} %pad_maximum_fusion.12), calls=%async_computation.1 | async-start | bytes 524288 | tf_op jit(solution)/shard_map/all_to_all | solution.py:153
  93.8 5.6 %collective-permute-start.8 = (f32[3,3,256]{2,1,0:T(4,128)S(1)}, f32[3,3,256]{2,1,0:T(4,128)S(1)}, u32[]{:S(2)}, u32[]{:S(2)}) collective-permute-start(f32[3,3,256]{2,1,0:T(4,128)S(1)} %slice_reduce_fusion), channel_id=1, source_target_pairs={{0,1},{2,3},{4,5},{6,7},{8,9},{10,11},{12,13},{14,15},{16,17},{18,... | collective-permute-start | bytes 27656 | tf_op jit(solution)/shard_map/ppermute | solution.py:29
  107.4 10.0 %collective-permute-start.9 = (f32[3,256,128]{2,1,0:T(8,128)S(1)}, f32[3,256,128]{2,1,0:T(8,128)S(1)}, u32[]{:S(2)}, u32[]{:S(2)}) collective-permute-start(f32[3,256,128]{2,1,0:T(8,128)S(1)} %slice_bitcast_fusion.2), channel_id=1, source_target_pairs={{0,2},{2,4},{4,6},{6,8},{8,10},{10,12},{12,14},{14,16},{16,18},{18... | collective-permute-start | bytes 1179656 | tf_op jit(solution)/shard_map/ppermute | solution.py:29
